TPU v7x, 256 devices: a whole 4x4x8 slice. The times are simulated.
256 devices in a mesh: batch: 64 (over y, x, z_hi), chan: 4 (over z_lo, core).
Axes of the slice: x: 4, y: 4, z: 8 (z_hi: 4, z_lo: 2; z = z_hi * 2 + z_lo), core: 2. Of those that a mesh axis runs over, the one named last changes fastest.
Arguments:
- fine_inputs: bfloat16 [64, 32, 32, 512], P('batch'), may hold values from -6 to 6
- fine_upstream: bfloat16 [64, 32, 32, 512], P('batch', None, None, 'chan'), may hold values from -6 to 6
- fine_bank: bfloat16 [8, 9, 512, 512], P(None, None, 'batch', 'chan'), may hold values from -0.09375 to 0.09375
- fine_coefs: float32 [64, 8], replicated, may hold values from 0 to 1, as said below
- coarse_inputs: bfloat16 [64, 16, 16, 512], P('batch'), may hold values from -6 to 6
- coarse_upstream: bfloat16 [64, 16, 16, 512], P('batch', None, None, 'chan'), may hold values from -6 to 6
- coarse_bank: bfloat16 [8, 9, 512, 512], P(None, None, 'batch', 'chan'), may hold values from -0.09375 to 0.09375
- coarse_coefs: float32 [64, 8], replicated, may hold values from 0 to 1, as said below
Outputs:
- fine_delta: bfloat16 [64, 32, 32, 512], P('batch', None, None, 'chan')
- fine_update: float32 [8, 9, 512, 512], P(None, None, 'batch', 'chan')
- fine_logit: float32 [64, 8], P('batch')
- coarse_delta: bfloat16 [64, 16, 16, 512], P('batch', None, None, 'chan')
- coarse_update: float32 [8, 9, 512, 512], P(None, None, 'batch', 'chan')
- coarse_logit: float32 [64, 8], P('batch')
Inputs may be any that keep to these rules, and one draw needn't show every extreme that they name: Each row of fine_coefs is a softmax: positive entries that sum to one. Each row of coarse_coefs is a softmax: positive entries that sum to one.
All inputs are finite; a program needn't handle non-finite values.
Results may differ from a plain program's by a relative error of at most 0.01.
Values may be sent and summed in bfloat16 or wider, within the bound.
A program may use at most 128 MiB of HBM per device.

v0:
```python
import jax
import jax.numpy as jnp
from jax import lax
from jax.sharding import PartitionSpec as P

BANKS = 8
FINE_SIDE = 32
COARSE_SIDE = 16
HIGH = lax.Precision.HIGHEST


def shifted(padded, row_shift, col_shift, side):
    window = padded[:, row_shift : row_shift + side, col_shift : col_shift + side, :]
    return window.reshape(window.shape[0], side * side, window.shape[3])


def local_grads(inputs, upstream, kernels, side):
    samples_here = inputs.shape[0]
    pad_in = jnp.pad(inputs, ((0, 0), (1, 1), (1, 1), (0, 0)))
    pad_up = jnp.pad(upstream, ((0, 0), (1, 1), (1, 1), (0, 0)))
    flat_up = upstream.reshape(samples_here, side * side, upstream.shape[3])
    delta = jnp.zeros((samples_here, side * side, inputs.shape[3]), jnp.float32)
    grad_taps = []
    for row_shift in range(3):
        for col_shift in range(3):
            tap = 3 * row_shift + col_shift
            window_in = shifted(pad_in, row_shift, col_shift, side)
            window_up = shifted(pad_up, 2 - row_shift, 2 - col_shift, side)
            grad_taps.append(
                jnp.einsum("bpc,bpo->bco", window_in, flat_up, preferred_element_type=jnp.float32)
                / side
            )
            delta = delta + jnp.einsum(
                "bpo,bco->bpc", window_up, kernels[:, tap], preferred_element_type=jnp.float32
            )
    return (delta.reshape(samples_here, side, side, inputs.shape[3]), jnp.stack(grad_taps, axis=1))


def one_layer(inputs, upstream, bank_part, coefs, side):
    samples_here = inputs.shape[0]
    first_row = lax.axis_index("batch") * samples_here
    own_coefs = lax.dynamic_slice_in_dim(coefs, first_row, samples_here, 0)
    flat_bank = bank_part.reshape(BANKS, -1).astype(jnp.float32)
    bank_rows = lax.all_gather(bank_part, "batch", axis=2, tiled=True)
    flat_rows = bank_rows.reshape(bank_rows.shape[0], -1).astype(jnp.float32)
    mixed = jnp.dot(own_coefs, flat_rows, precision=HIGH)
    kernels = mixed.reshape((samples_here,) + bank_rows.shape[1:]).astype(jnp.bfloat16)
    delta, kernel_grad = local_grads(inputs, upstream, kernels, side)
    delta_total = lax.psum(delta.astype(jnp.bfloat16), "chan").astype(jnp.float32)
    width = delta.shape[3] // lax.axis_size("chan")
    delta_part = lax.dynamic_slice_in_dim(delta_total, lax.axis_index("chan") * width, width, 3)
    moved = lax.all_to_all(
        kernel_grad.astype(jnp.bfloat16), "batch", split_axis=2, concat_axis=0, tiled=True
    ).astype(kernel_grad.dtype)
    flat_grads = moved.reshape(moved.shape[0], -1)
    update = jnp.dot(coefs.T, flat_grads, precision=HIGH).reshape(bank_part.shape)
    dcoef_part = lax.dot_general(flat_grads, flat_bank, (((1,), (1,)), ((), ())), precision=HIGH)
    return (delta_part.astype(jnp.bfloat16), update, dcoef_part)


def logit_grads(coefs, totals, samples_here):
    first_row = lax.axis_index("batch") * samples_here
    own_coefs = lax.dynamic_slice_in_dim(coefs, first_row, samples_here, 0)
    own_totals = lax.dynamic_slice_in_dim(totals, first_row, samples_here, 0)
    return own_coefs * (own_totals - jnp.sum(own_coefs * own_totals, axis=1, keepdims=True))


def per_device(
    fine_inputs,
    fine_upstream,
    fine_bank,
    fine_coefs,
    coarse_inputs,
    coarse_upstream,
    coarse_bank,
    coarse_coefs,
):
    fine_delta, fine_update, fine_partial = one_layer(
        fine_inputs, fine_upstream, fine_bank, fine_coefs, FINE_SIDE
    )
    coarse_delta, coarse_update, coarse_partial = one_layer(
        coarse_inputs, coarse_upstream, coarse_bank, coarse_coefs, COARSE_SIDE
    )
    fine_total, coarse_total = lax.psum((fine_partial, coarse_partial), ("batch", "chan"))
    samples_here = fine_inputs.shape[0]
    fine_logit = logit_grads(fine_coefs, fine_total, samples_here)
    coarse_logit = logit_grads(coarse_coefs, coarse_total, samples_here)
    return (fine_delta, fine_update, fine_logit, coarse_delta, coarse_update, coarse_logit)


def solution(mesh):
    return jax.shard_map(
        per_device,
        mesh=mesh,
        in_specs=(
            P("batch", None, None, None),
            P("batch", None, None, "chan"),
            P(None, None, "batch", "chan"),
            P(),
            P("batch", None, None, None),
            P("batch", None, None, "chan"),
            P(None, None, "batch", "chan"),
            P(),
        ),
        out_specs=(
            P("batch", None, None, "chan"),
            P(None, None, "batch", "chan"),
            P("batch", None),
            P("batch", None, None, "chan"),
            P(None, None, "batch", "chan"),
            P("batch", None),
        ),
        check_vma=False,
    )
```

profile of v0, /device:TPU:1, one launch (start us, length us, event | category | flops | bytes accessed | tf_op | source)
XLA Modules:
  0.0 524.2 jit_solution(8585332356747162847)
XLA Ops:
  7.2 0.7 all-gather.5.cloned.1.call-update
  8.0 0.7 all-gather.3.cloned.1.call-update
  8.7 1.2 fusion.60
  12.3 2.2 copy.31
  14.5 15.2 %all-to-all-start.1 = ((bf16[1,9,512,128]{3,1,0,2:T(8,128)(2,1)}), bf16[1,9,512,128]{3,1,0,2:T(8,128)(2,1)S(1)}, u32[]{:S(2)}, u32[]{:S(2)}) async-start(bf16[1,9,512,128]{3,1,0,2:T(8,128)(2,1)} %copy.31), calls=%async_computation.1 | async-start | bytes 4194304 | tf_op jit(solution)/shard_map/all_to_all | solution.py:52
  30.3 0.5 fusion.76
  30.8 0.5 fusion.74
  31.4 0.5 fusion.72
  31.9 0.5 fusion.70
  32.5 0.5 fusion.68
  33.0 0.6 fusion.66
  33.6 0.5 fusion.64
  34.1 0.5 fusion.62
  34.7 2.2 copy.28
  36.9 51.0 %all-to-all-done.1 = bf16[1,9,512,128]{3,1,0,2:T(8,128)(2,1)S(1)} async-done(((bf16[1,9,512,128]{3,1,0,2:T(8,128)(2,1)}), bf16[1,9,512,128]{3,1,0,2:T(8,128)(2,1)S(1)}, u32[]{:S(2)}, u32[]{:S(2)}) %all-to-all-start.1) | async-done | bytes 1179680 | tf_op jit(solution)/shard_map/all_to_all | solution.py:52
  87.9 5.9 %all-to-all-start = ((bf16[1,9,512,128]{3,1,0,2:T(8,128)(2,1)}), bf16[1,9,512,128]{3,1,0,2:T(8,128)(2,1)}, u32[]{:S(2)}, u32[]{:S(2)}) async-start(bf16[1,9,512,128]{3,1,0,2:T(8,128)(2,1)} %copy.28), calls=%async_computation | async-start | bytes 4194304 | tf_op jit(solution)/shard_map/all_to_all | solution.py:52
  94.1 0.6 copy.41
  94.7 0.6 copy.40
  95.3 0.8 pad_slice_fusion.24
  96.1 1.3 pad_slice_fusion.16
  97.8 1.3 reshape.891
  99.1 48.8 %all-to-all-done = bf16[1,9,512,128]{3,1,0,2:T(8,128)(2,1)} async-done(((bf16[1,9,512,128]{3,1,0,2:T(8,128)(2,1)}), bf16[1,9,512,128]{3,1,0,2:T(8,128)(2,1)}, u32[]{:S(2)}, u32[]{:S(2)}) %all-to-all-start) | async-done | bytes 1179680 | tf_op jit(solution)/shard_map/all_to_all | solution.py:52
  148.0 2.0 copy.61
  150.0 0.5 reshape.858
  150.5 0.6 fusion.166
  151.1 80.3 %all-gather.5.cloned.1.call-done = bf16[8,9,512,128]{3,2,1,0:T(8,128)(2,1)} async-done(((bf16[8,9,8,128]{3,2,1,0:T(8,128)(2,1)}), bf16[8,9,512,128]{3,2,1,0:T(8,128)(2,1)}) %all-gather.5.cloned.1.call-update) | async-done | bytes 9437200 | tf_op jit(solution)/shard_map/all_gather | solution.py:44
  231.4 16.2 %copy.58 = bf16[1,8,4608,128]{3,1,2,0:T(8,128)(2,1)S(1)} copy(bf16[1,8,4608,128]{3,2,1,0:T(8,128)(2,1)} %bitcast.537) | data formatting | bytes 18874368
  247.6 8.0 %fusion.146 = f32[1,9,512,128]{3,0,2,1:T(1,128)S(1)} fusion(bf16[9,512,128,8]{2,3,1,0:T(8,128)(2,1)S(1)} %bitcast.532, f32[1,8]{0,1:T(8,128)S(1)} %get-tuple-element.44), kind=kOutput, calls=%fused_computation.215 | convolution fusion | flops 56623104 | bytes 11796512 | tf_op jit(solution)/shard_map/dot_general | solution.py:46
  255.8 136.1 %all-gather.3.cloned.1.call-done = bf16[8,9,512,128]{3,2,1,0:T(8,128)(2,1)} async-done(((bf16[8,9,8,128]{3,2,1,0:T(8,128)(2,1)}), bf16[8,9,512,128]{3,2,1,0:T(8,128)(2,1)}) %all-gather.3.cloned.1.call-update) | async-done | bytes 9437200 | tf_op jit(solution)/shard_map/all_gather | solution.py:44
  391.9 16.2 %copy.59 = bf16[1,8,4608,128]{3,1,2,0:T(8,128)(2,1)S(1)} copy(bf16[1,8,4608,128]{3,2,1,0:T(8,128)(2,1)} %bitcast.536) | data formatting | bytes 18874368
  408.1 8.3 %fusion.148 = f32[1,9,512,128]{3,0,2,1:T(1,128)S(1)} fusion(bf16[9,512,128,8]{2,3,1,0:T(8,128)(2,1)S(1)} %bitcast.533, f32[1,8]{0,1:T(8,128)S(1)} %get-tuple-element.45), kind=kOutput, calls=%fused_computation.217 | convolution fusion | flops 56623104 | bytes 11796512 | tf_op jit(solution)/shard_map/dot_general | solution.py:46
  416.6 0.8 copy-done.9
  417.8 0.5 copy-done.8
  418.7 0.5 copy-done.7
  419.7 0.5 copy-done.6
  427.9 0.9 fusion.6
  428.8 1.9 fusion.4
  430.7 1.2 copy-done
  432.0 0.6 fusion.167
  432.5 0.8 copy.33
  433.3 0.8 copy.34
  435.0 76.0 %all-reduce.4 = (f32[64,8]{1,0:T(8,128)S(1)}, f32[64,8]{1,0:T(8,128)S(1)}) all-reduce(f32[64,8]{1,0:T(8,128)S(1)} %fusion.125, f32[64,8]{1,0:T(8,128)S(1)} %fusion.122), channel_id=1, replica_groups=mesh['batch'=64,'chan'=4] {'batch','chan'}, use_global_device_ids=true, to_apply=%region_1.2 | all-reduce | flops 1024 | bytes 8192 | tf_op jit(solution)/shard_map/psum | solution.py:84
  511.0 0.6 multiply_reduce_fusion
  511.6 0.6 multiply_reduce_fusion.1
  512.2 1.2 subtract_multiply_fusion
  513.3 1.2 subtract_multiply_fusion.1
  514.5 1.7 convert_convert_fusion
  516.2 1.5 convert_convert_fusion.1
  (87 shorter events, 13.6 us)
Async XLA Ops:
  7.2 2.8 copy-start.10
  7.2 2.7 copy-start.27
  7.2 224.2 %all-gather.5.cloned.1.call-start = ((), (), s32[]{:S(2)}) async-start(), calls=%async_computation.3 | async-start | bytes 9584640 | tf_op jit(solution)/shard_map/all_gather | solution.py:44
  7.9 384.0 %all-gather.3.cloned.1.call-start = ((), (), s32[]{:S(2)}) async-start(), calls=%async_computation.2 | async-start | bytes 9584640 | tf_op jit(solution)/shard_map/all_gather | solution.py:44
  14.5 15.3 %copy-start.1 = (bf16[1,32,32,128]{3,2,1,0:T(8,128)(2,1)S(1)}, bf16[1,32,32,128]{3,2,1,0:T(8,128)(2,1)}, u32[]{:S(2)}) copy-start(bf16[1,32,32,128]{3,2,1,0:T(8,128)(2,1)} %param.9) | copy-start | bytes 786436
  14.5 15.3 %copy-start.26 = (bf16[1,32,32,512]{3,2,1,0:T(8,128)(2,1)S(1)}, bf16[1,32,32,512]{3,2,1,0:T(8,128)(2,1)}, u32[]{:S(2)}) copy-start(bf16[1,32,32,512]{3,2,1,0:T(8,128)(2,1)} %param.8) | copy-start | bytes 3145732
  14.5 73.4 %all-to-all-start.1 = ((bf16[1,9,512,128]{3,1,0,2:T(8,128)(2,1)}), bf16[1,9,512,128]{3,1,0,2:T(8,128)(2,1)S(1)}, u32[]{:S(2)}, u32[]{:S(2)}) async-start(bf16[1,9,512,128]{3,1,0,2:T(8,128)(2,1)} %copy.31), calls=%async_computation.1 | async-start | bytes 4194304 | tf_op jit(solution)/shard_map/all_to_all | solution.py:52
  36.9 57.2 %copy-start.22 = (f32[64,8]{0,1:T(8,128)S(1)}, f32[64,8]{0,1:T(8,128)}, u32[]{:S(2)}) copy-start(f32[64,8]{0,1:T(8,128)} %param.11) | copy-start | bytes 6148
  36.9 57.2 %copy-start.23 = (f32[64,8]{0,1:T(8,128)S(1)}, f32[64,8]{0,1:T(8,128)}, u32[]{:S(2)}) copy-start(f32[64,8]{0,1:T(8,128)} %param.15) | copy-start | bytes 6148
  87.9 60.1 %all-to-all-start = ((bf16[1,9,512,128]{3,1,0,2:T(8,128)(2,1)}), bf16[1,9,512,128]{3,1,0,2:T(8,128)(2,1)}, u32[]{:S(2)}, u32[]{:S(2)}) async-start(bf16[1,9,512,128]{3,1,0,2:T(8,128)(2,1)} %copy.28), calls=%async_computation | async-start | bytes 4194304 | tf_op jit(solution)/shard_map/all_to_all | solution.py:52
  93.8 420.7 %all-reduce.8.cloned.1.call-start = ((), (), s32[]{:S(2)}) async-start(), calls=%async_computation.4 | async-start | bytes 2621440 | tf_op jit(solution)/shard_map/psum | solution.py:49
  416.4 1.0 copy-start.9
  417.3 0.9 copy-start.8
  418.3 0.9 copy-start.7
  419.2 0.9 copy-start.6
  420.2 0.9 copy-start.5
  421.1 0.9 copy-start.4
  422.1 0.9 copy-start.3
  423.0 0.9 copy-start.2
  424.0 0.8 copy-start.18
  424.0 1.1 copy-start.17
  424.4 0.9 copy-start.16
  425.1 0.8 copy-start.15
  425.3 0.8 copy-start.11
  425.9 0.8 copy-start.14
  426.2 0.8 copy-start.13
  426.8 0.8 copy-start.12
  427.0 0.8 copy-start.19
  430.7 1.3 copy-start
  431.9 2.1 copy-start.20
  433.3 1.2 copy-start.21
  434.5 76.4 %copy-start.25 = (f32[1,8]{1,0:T(1,128)S(1)}, f32[1,8]{1,0:T(1,128)}, u32[]{:S(2)}) copy-start(f32[1,8]{1,0:T(1,128)} %copy.41) | copy-start | bytes 100
  434.5 77.0 %copy-start.24 = (f32[1,8]{1,0:T(1,128)S(1)}, f32[1,8]{1,0:T(1,128)}, u32[]{:S(2)}) copy-start(f32[1,8]{1,0:T(1,128)} %copy.40) | copy-start | bytes 100
Sparse Core Ops, SparseCore 0:
  11.1 220.1 all-gather.4
  234.5 157.3 all-gather.2
  430.8 49.6 all-reduce.7
where the time goes:
time: 525 us; the launch traced here: 524 us
  waiting for transfers between devices  318 us (61%)
  blocking collectives  76 us (14%)
  local copies, waits for them, and re-layouts  53.3 us (10%)
  matrix products  34.7 us (7%)
  starting transfers between devices  21.4 us (4%)
  between operations  14.2 us (3%)
  other arithmetic  7.02 us (1%)
    all_gather x2, waiting for transfers between devices, one_layer(): bank_rows = lax.all_gather(bank_part, 'batch', axis=2, tiled=True)  216 us
    all_to_all x2, waiting for transfers between devices, one_layer(): lax.all_to_all(kernel_grad.astype(jnp.bfloat16), 'batch', split_axis=2, c...  99.9 us
    psum x1, blocking collectives, per_device(): lax.psum((fine_partial, coarse_partial), ('batch', 'chan'))  76 us
    unnamed x62, local copies, waits for them, and re-layouts  42.3 us
    all_to_all x2, starting transfers between devices, one_layer(): lax.all_to_all(kernel_grad.astype(jnp.bfloat16), 'batch', split_axis=2, c...  21.1 us
    dot_general x2, matrix products, one_layer(): mixed = jnp.dot(own_coefs, flat_rows, precision=HIGH)  16.3 us
  transfers between devices with their start and end apart: 5, of which 4 were waited for; matrix products, arithmetic and copies ran while one was open for 10% of the time, Pallas kernels for 0%

commit v1 on v0

--- a/solution.py
+++ b/solution.py
@@ -49,9 +49,11 @@
     delta_total = lax.psum(delta.astype(jnp.bfloat16), "chan").astype(jnp.float32)
     width = delta.shape[3] // lax.axis_size("chan")
     delta_part = lax.dynamic_slice_in_dim(delta_total, lax.axis_index("chan") * width, width, 3)
-    moved = lax.all_to_all(
-        kernel_grad.astype(jnp.bfloat16), "batch", split_axis=2, concat_axis=0, tiled=True
-    ).astype(kernel_grad.dtype)
+    build_block = lambda xs, dim_i, array_axis: jnp.concatenate(
+        lax.all_to_all(jnp.stack(jnp.split(xs, lax.axis_size("batch"), axis=dim_i)), "batch", 0, 0),
+        axis=array_axis,
+    )
+    moved = build_block(kernel_grad.astype(jnp.bfloat16), 2, 0).astype(kernel_grad.dtype)
     flat_grads = moved.reshape(moved.shape[0], -1)
     update = jnp.dot(coefs.T, flat_grads, precision=HIGH).reshape(bank_part.shape)
     dcoef_part = lax.dot_general(flat_grads, flat_bank, (((1,), (1,)), ((), ())), precision=HIGH)

time: 525 us -> 506 us (0.964)
  waiting for transfers between devices: 318 us -> 224 us
  local copies, waits for them, and re-layouts: 53.3 us -> 121 us
  starting transfers between devices: 21.4 us -> 27.5 us
    all_to_all x2, waiting for transfers between devices: 99.9 us -> 0.01 us  [one_layer(): lax.all_to_all(jnp.stack(jnp.split(xs, lax.axis_size('batch'), axis=dim_i...]
    unnamed x62 -> x186, local copies, waits for them, and re-layouts: 42.3 us -> 118 us
    all_to_all x2, starting transfers between devices: 21.1 us -> 27.4 us  [one_layer(): lax.all_to_all(jnp.stack(jnp.split(xs, lax.axis_size('batch'), axis=dim_i...]
    all_gather x2, waiting for transfers between devices: 216 us -> 222 us  [one_layer(): bank_rows = lax.all_gather(bank_part, 'batch', axis=2, tiled=True)]
  transfers between devices with their start and end apart: 5 -> 5, of which waited for: 4 -> 2; matrix products, arithmetic and copies ran while one was open for 10% -> 30% of each run, Pallas kernels for 0% -> 0%
where the time goes in v1:
time: 506 us; the launch traced here: 505 us
  waiting for transfers between devices  224 us (44%)
  local copies, waits for them, and re-layouts  121 us (24%)
  blocking collectives  75.9 us (15%)
  matrix products  35.6 us (7%)
  starting transfers between devices  27.5 us (5%)
  between operations  14.3 us (3%)
  other arithmetic  7.02 us (1%)
    all_gather x2, waiting for transfers between devices, one_layer(): bank_rows = lax.all_gather(bank_part, 'batch', axis=2, tiled=True)  222 us
    unnamed x186, local copies, waits for them, and re-layouts  118 us
    psum x1, blocking collectives, per_device(): lax.psum((fine_partial, coarse_partial), ('batch', 'chan'))  75.9 us
    all_to_all x2, starting transfers between devices, one_layer(): lax.all_to_all(jnp.stack(jnp.split(xs, lax.axis_size('batch'), axis=dim_i...  27.4 us
    dot_general x2, matrix products, one_layer(): mixed = jnp.dot(own_coefs, flat_rows, precision=HIGH)  16.3 us
  transfers between devices with their start and end apart: 5, of which 2 were waited for; matrix products, arithmetic and copies ran while one was open for 30% of the time, Pallas kernels for 0%

profile of v1, /device:TPU:1, one launch (start us, length us, event | category | flops | bytes accessed | tf_op | source)
XLA Modules:
  0.0 505.0 jit_solution(9787268613415035324)
XLA Ops:
  7.2 0.7 all-gather.5.cloned.1.call-update
  8.0 0.7 all-gather.3.cloned.1.call-update
  8.7 1.2 fusion.68
  14.2 0.6 constant_dynamic-update-slice_fusion.124
  14.8 0.6 constant_dynamic-update-slice_fusion.123
  18.4 0.6 constant_dynamic-update-slice_fusion.117
  24.5 0.6 constant_dynamic-update-slice_fusion.107
  31.8 0.6 constant_dynamic-update-slice_fusion.95
  38.4 0.6 constant_dynamic-update-slice_fusion.84
  50.5 0.6 constant_dynamic-update-slice_fusion.64
  51.1 15.2 %all-to-all-start.1 = ((bf16[64,1,9,8,128]{4,3,2,1,0:T(8,128)(2,1)}), bf16[64,1,9,8,128]{4,3,2,1,0:T(8,128)(2,1)S(1)}, u32[]{:S(2)}, u32[]{:S(2)}) async-start(bf16[64,1,9,8,128]{4,3,2,1,0:T(8,128)(2,1)} %constant_dynamic-update-slice_fusion.64), calls=%async_computation.1 | async-start | bytes 2359296 | tf_op jit(solution)/shard_map/all_to_all | solution.py:53
  66.7 1.4 pad_slice_fusion.16
  73.5 0.6 constant_dynamic-update-slice_fusion.63
  75.3 0.6 constant_dynamic-update-slice_fusion.60
  78.4 0.6 constant_dynamic-update-slice_fusion.55
  80.2 0.6 constant_dynamic-update-slice_fusion.52
  81.4 0.6 constant_dynamic-update-slice_fusion.50
  85.7 0.6 constant_dynamic-update-slice_fusion.43
  86.3 0.6 constant_dynamic-update-slice_fusion.42
  89.9 0.6 constant_dynamic-update-slice_fusion.36
  91.1 0.6 constant_dynamic-update-slice_fusion.34
  95.4 0.6 constant_dynamic-update-slice_fusion.27
  97.2 0.6 constant_dynamic-update-slice_fusion.24
  99.0 0.6 constant_dynamic-update-slice_fusion.21
  100.8 0.6 constant_dynamic-update-slice_fusion.18
  106.3 0.8 pad_slice_fusion.24
  107.1 0.6 constant_dynamic-update-slice_fusion.9
  108.9 0.6 constant_dynamic-update-slice_fusion.6
  111.3 0.6 constant_dynamic-update-slice_fusion.2
  112.5 0.6 constant_dynamic-update-slice_fusion
  113.2 12.2 %all-to-all-start = ((bf16[64,1,9,8,128]{4,3,2,1,0:T(8,128)(2,1)}), bf16[64,1,9,8,128]{4,3,2,1,0:T(8,128)(2,1)S(1)}, u32[]{:S(2)}, u32[]{:S(2)}) async-start(bf16[64,1,9,8,128]{4,3,2,1,0:T(8,128)(2,1)} %constant_dynamic-update-slice_fusion), calls=%async_computation | async-start | bytes 2359296 | tf_op jit(solution)/shard_map/all_to_all | solution.py:53
  125.4 1.3 fusion.9
  126.7 87.5 %all-gather.5.cloned.1.call-done = bf16[8,9,512,128]{3,2,1,0:T(8,128)(2,1)} async-done(((bf16[8,9,8,128]{3,2,1,0:T(8,128)(2,1)}), bf16[8,9,512,128]{3,2,1,0:T(8,128)(2,1)}) %all-gather.5.cloned.1.call-update) | async-done | bytes 9437200 | tf_op jit(solution)/shard_map/all_gather | solution.py:44
  214.2 16.2 %copy.58 = bf16[1,8,4608,128]{3,1,2,0:T(8,128)(2,1)S(1)} copy(bf16[1,8,4608,128]{3,2,1,0:T(8,128)(2,1)} %bitcast.1043) | data formatting | bytes 18874368
  230.4 8.0 %fusion.156 = f32[1,9,512,128]{3,0,2,1:T(1,128)S(1)} fusion(bf16[9,512,128,8]{2,3,1,0:T(8,128)(2,1)S(1)} %bitcast.1038, f32[1,8]{0,1:T(8,128)S(1)} %get-tuple-element.32), kind=kOutput, calls=%fused_computation.479 | convolution fusion | flops 56623104 | bytes 11796512 | tf_op jit(solution)/shard_map/dot_general | solution.py:46
  238.7 134.7 %all-gather.3.cloned.1.call-done = bf16[8,9,512,128]{3,2,1,0:T(8,128)(2,1)} async-done(((bf16[8,9,8,128]{3,2,1,0:T(8,128)(2,1)}), bf16[8,9,512,128]{3,2,1,0:T(8,128)(2,1)}) %all-gather.3.cloned.1.call-update) | async-done | bytes 9437200 | tf_op jit(solution)/shard_map/all_gather | solution.py:44
  373.3 16.2 %copy.59 = bf16[1,8,4608,128]{3,1,2,0:T(8,128)(2,1)S(1)} copy(bf16[1,8,4608,128]{3,2,1,0:T(8,128)(2,1)} %bitcast.1042) | data formatting | bytes 18874368
  389.6 8.3 %fusion.158 = f32[1,9,512,128]{3,0,2,1:T(1,128)S(1)} fusion(bf16[9,512,128,8]{2,3,1,0:T(8,128)(2,1)S(1)} %bitcast.1039, f32[1,8]{0,1:T(8,128)S(1)} %get-tuple-element.33), kind=kOutput, calls=%fused_computation.481 | convolution fusion | flops 56623104 | bytes 11796512 | tf_op jit(solution)/shard_map/dot_general | solution.py:46
  398.0 0.8 copy-done.10
  404.6 0.9 fusion.6
  410.3 1.9 fusion.4
  413.1 0.8 copy.18
  413.9 0.8 copy.17
  416.0 75.9 %all-reduce.4 = (f32[64,8]{1,0:T(8,128)S(1)}, f32[64,8]{1,0:T(8,128)S(1)}) all-reduce(f32[64,8]{1,0:T(8,128)S(1)} %fusion.11, f32[64,8]{1,0:T(8,128)S(1)} %fusion.7), channel_id=1, replica_groups=mesh['batch'=64,'chan'=4] {'batch','chan'}, use_global_device_ids=true, to_apply=%region_1.2 | all-reduce | flops 1024 | bytes 8192 | tf_op jit(solution)/shard_map/psum | solution.py:86
  493.0 1.2 subtract_multiply_fusion
  494.2 1.2 subtract_multiply_fusion.1
  495.4 1.7 convert_convert_fusion
  497.0 1.5 convert_convert_fusion.1
  (207 shorter events, 85.2 us)
Async XLA Ops:
  7.2 2.8 copy-start.26
  7.2 2.8 copy-start.11
  7.2 207.0 %all-gather.5.cloned.1.call-start = ((), (), s32[]{:S(2)}) async-start(), calls=%async_computation.3 | async-start | bytes 9584640 | tf_op jit(solution)/shard_map/all_gather | solution.py:44
  7.9 365.4 %all-gather.3.cloned.1.call-start = ((), (), s32[]{:S(2)}) async-start(), calls=%async_computation.2 | async-start | bytes 9584640 | tf_op jit(solution)/shard_map/all_gather | solution.py:44
  51.1 15.3 %copy-start.23 = (f32[64,8]{0,1:T(8,128)S(1)}, f32[64,8]{0,1:T(8,128)}, u32[]{:S(2)}) copy-start(f32[64,8]{0,1:T(8,128)} %param.15) | copy-start | bytes 6148
  51.1 15.3 %copy-start.24 = (f32[64,8]{0,1:T(8,128)S(1)}, f32[64,8]{0,1:T(8,128)}, u32[]{:S(2)}) copy-start(f32[64,8]{0,1:T(8,128)} %param.11) | copy-start | bytes 6148
  51.1 15.5 %copy-start.2 = (bf16[1,32,32,128]{3,2,1,0:T(8,128)(2,1)S(1)}, bf16[1,32,32,128]{3,2,1,0:T(8,128)(2,1)}, u32[]{:S(2)}) copy-start(bf16[1,32,32,128]{3,2,1,0:T(8,128)(2,1)} %param.9) | copy-start | bytes 786436
  51.1 62.0 %all-to-all-start.1 = ((bf16[64,1,9,8,128]{4,3,2,1,0:T(8,128)(2,1)}), bf16[64,1,9,8,128]{4,3,2,1,0:T(8,128)(2,1)S(1)}, u32[]{:S(2)}, u32[]{:S(2)}) async-start(bf16[64,1,9,8,128]{4,3,2,1,0:T(8,128)(2,1)} %constant_dynamic-update-slice_fusion.64), calls=%async_computation.1 | async-start | bytes 2359296 | tf_op jit(solution)/shard_map/all_to_all | solution.py:53
  66.6 1.9 copy-start.25
  113.2 299.0 %all-to-all-start = ((bf16[64,1,9,8,128]{4,3,2,1,0:T(8,128)(2,1)}), bf16[64,1,9,8,128]{4,3,2,1,0:T(8,128)(2,1)S(1)}, u32[]{:S(2)}, u32[]{:S(2)}) async-start(bf16[64,1,9,8,128]{4,3,2,1,0:T(8,128)(2,1)} %constant_dynamic-update-slice_fusion), calls=%async_computation | async-start | bytes 2359296 | tf_op jit(solution)/shard_map/all_to_all | solution.py:53
  125.3 370.0 %all-reduce.8.cloned.1.call-start = ((), (), s32[]{:S(2)}) async-start(), calls=%async_computation.4 | async-start | bytes 2621440 | tf_op jit(solution)/shard_map/psum | solution.py:49
  397.8 1.0 copy-start.10
  398.8 0.9 copy-start.9
  399.7 0.9 copy-start.8
  400.7 0.8 copy-start.19
  400.7 1.1 copy-start.18
  401.1 0.9 copy-start.17
  401.8 0.8 copy-start.16
  402.0 0.8 copy-start.12
  402.6 0.8 copy-start.15
  402.9 0.8 copy-start.14
  403.5 0.8 copy-start.13
  403.7 0.8 copy-start.20
  404.0 1.6 copy-start.7
  405.5 1.0 copy-start.6
  406.5 0.9 copy-start.5
  407.4 0.9 copy-start.4
  408.4 0.9 copy-start.3
  409.3 0.9 copy-start.1
  412.1 1.0 copy-start
  412.2 2.5 copy-start.21
  414.6 0.9 copy-start.22
Sparse Core Ops, SparseCore 0:
  11.1 203.0 all-gather.4
  217.3 155.9 all-gather.2
  412.3 49.6 all-reduce.7
